TPU v7x, 512 devices: a whole 4x8x8 slice. The times are simulated.
512 devices in a mesh: dp: 16 (over y, core), tensor: 32 (over z, x).
Axes of the slice: x: 4, y: 8, z: 8, core: 2. Of those that a mesh axis runs over, the one named last changes fastest.
Arguments:
- tokens: bfloat16 [2048, 4096], P('dp', 'tensor'), may hold values from -6 to 6
- gate_pre: bfloat16 [2048, 16384], P('dp', 'tensor'), may hold values from -6 to 6
- up_blocks: bfloat16 [32, 64, 128, 128], P('tensor'), may hold values from -0.125 to 0.125
- up_mask: int32 [32, 128], P(None, 'tensor'), may hold values from 0 to 1, as said below
- down_blocks: bfloat16 [32, 64, 128, 128], P('tensor'), may hold values from -0.0625 to 0.0625
- down_mask: int32 [128, 32], replicated, may hold values from 0 to 1, as said below
- down_owner: int32 [128], replicated, may hold values from 0 to 31, as said below
- cotangent: bfloat16 [2048, 4096], P('dp', 'tensor'), may hold values from -6 to 6
Outputs:
- mixed: bfloat16 [2048, 4096], P('dp', 'tensor')
- input_grad: bfloat16 [2048, 4096], P('dp', 'tensor')
- gate_grad: bfloat16 [2048, 16384], P('dp', 'tensor')
- up_grad: bfloat16 [32, 64, 128, 128], P('tensor', 'dp')
- down_grad: bfloat16 [32, 64, 128, 128], P('tensor', 'dp')
Inputs may be any that keep to these rules, and one draw needn't show every extreme that they name: `up_mask`: each column strip of 4 block columns holds exactly 64 ones. `down_mask`: the rows owned by one device hold exactly 64 ones together. `down_owner`: every device owns exactly 4 block rows.
All inputs are finite; a program needn't handle non-finite values.
Results may differ from a plain program's by a relative error of at most 0.022.
Values may be sent and summed in bfloat16 or wider, within the bound.
No kernel may reach another device: no remote copies, remote signals or barrier semaphores. Data moves between devices by JAX's collectives and lax.ppermute only.
A program may use at most 128 MiB of HBM per device.

v0:
```python
import jax
import jax.numpy as jnp
from jax import lax
from jax.sharding import PartitionSpec as P


def kept_positions(marked, total):
    marked = marked.reshape(-1).astype(jnp.int32)
    running = jnp.cumsum(marked) - 1
    target = jnp.where(marked > 0, running, total)
    indices = jnp.arange(marked.shape[0], dtype=jnp.int32)
    return jnp.zeros((total,), jnp.int32).at[target].set(indices, mode="drop")


def one_hot(indices, total):
    return (indices[:, None] == jnp.arange(total, dtype=jnp.int32)[None, :]).astype(jnp.float32)


def row_slots(down_owner, devices):
    marks = (down_owner[:, None] == jnp.arange(devices, dtype=jnp.int32)[None, :]).astype(jnp.int32)
    earlier = jnp.cumsum(marks, axis=0) - marks
    return jnp.sum(earlier * marks, axis=1)


def picker(wanted, block, current, segment):
    block_count = segment.shape[1] // block
    inside = (wanted >= 0) & (wanted < block_count)
    shaped = segment.reshape(segment.shape[0], block_count, block)
    chosen = jnp.take(shaped, jnp.clip(wanted, 0, block_count - 1), axis=1)
    return jnp.where(inside[None, :, None], chosen, current)


def shards(tokens, gate_pre, up_blocks, up_mask, down_blocks, down_mask, down_owner, cotangent):
    devices = lax.axis_size("tensor")
    position = lax.axis_index("tensor")
    token_count = tokens.shape[0]
    blocks_wide = up_mask.shape[0]
    strip_size = up_mask.shape[1]
    block = up_blocks.shape[2]
    kept_up = up_blocks.shape[1]
    kept_down = down_blocks.shape[1]
    model_width = blocks_wide * block
    highest = lax.Precision.HIGHEST
    x_full, dy_full = (
        lax.all_gather(tokens, "tensor", axis=1, tiled=True),
        lax.all_gather(cotangent, "tensor", axis=1, tiled=True),
    )
    token_blocks = x_full.reshape(token_count, blocks_wide, block)
    cot_blocks = dy_full.reshape(token_count, blocks_wide, block)
    w_up = up_blocks[0]
    w_down = down_blocks[0]
    up_pos = kept_positions(up_mask, kept_up)
    up_rows = up_pos // strip_size
    up_cols = up_pos % strip_size
    token_chosen = jnp.take(token_blocks, up_rows, axis=1)
    product = jnp.einsum("nkb,kbc->nkc", token_chosen, w_up, preferred_element_type=jnp.float32)
    up_val = jnp.einsum("nkc,ks->nsc", product, one_hot(up_cols, strip_size), precision=highest)
    gate_val = gate_pre.reshape(token_count, strip_size, block).astype(jnp.float32)
    sigmoid_gate = jax.nn.sigmoid(gate_val)
    activated = gate_val * sigmoid_gate
    hidden = (activated * up_val).astype(jnp.bfloat16).reshape(token_count, strip_size * block)
    my_rows = kept_positions(down_owner == position, strip_size)
    owned_mask = jnp.take(down_mask, my_rows, axis=0)
    down_pos = kept_positions(owned_mask, kept_down)
    slots = down_pos // blocks_wide
    down_cols = down_pos % blocks_wide
    empty = jnp.zeros((token_count, strip_size, block), jnp.bfloat16)
    hidden_owned = picker(
        my_rows, block, empty, lax.all_gather(hidden, "tensor", axis=1, tiled=True)
    )
    h_chosen = jnp.take(hidden_owned, slots, axis=1)
    product = jnp.einsum("nkb,kbc->nkc", h_chosen, w_down, preferred_element_type=jnp.float32)
    out_part = jnp.einsum(
        "nkc,kj->njc", product, one_hot(down_cols, blocks_wide), precision=highest
    )
    out_part = out_part.astype(jnp.bfloat16).reshape(1, token_count, model_width)
    dy_chosen = jnp.take(cot_blocks, down_cols, axis=1)
    down_term = jnp.einsum("nkb,nkc->kbc", h_chosen, dy_chosen, preferred_element_type=jnp.float32)[
        None
    ]
    backward = jnp.einsum("nkc,kbc->nkb", dy_chosen, w_down, preferred_element_type=jnp.float32)
    dh_owned = jnp.einsum("nkb,ka->nab", backward, one_hot(slots, strip_size), precision=highest)
    dh_owned = dh_owned.astype(jnp.bfloat16).reshape(token_count, strip_size * block)
    home_index = down_owner * strip_size + row_slots(down_owner, devices)
    targets = position * strip_size + jnp.arange(strip_size, dtype=jnp.int32)
    wanted = jnp.take(home_index, targets)
    hidden_grad = picker(
        wanted, block, empty, lax.all_gather(dh_owned, "tensor", axis=1, tiled=True)
    )
    dh_float = hidden_grad.astype(jnp.float32)
    gate_grad = (dh_float * up_val * sigmoid_gate * (1.0 + gate_val * (1.0 - sigmoid_gate))).astype(
        jnp.bfloat16
    )
    gate_grad = gate_grad.reshape(token_count, strip_size * block)
    up_act_grad = (dh_float * activated).astype(jnp.bfloat16)
    du_chosen = jnp.take(up_act_grad, up_cols, axis=1)
    product = jnp.einsum("nkc,kbc->nkb", du_chosen, w_up, preferred_element_type=jnp.float32)
    in_part = jnp.einsum("nkb,kr->nrb", product, one_hot(up_rows, blocks_wide), precision=highest)
    in_part = in_part.astype(jnp.bfloat16).reshape(1, token_count, model_width)
    up_term = jnp.einsum(
        "nkb,nkc->kbc", token_chosen, du_chosen, preferred_element_type=jnp.float32
    )[None]
    out_pieces, in_pieces = (
        lax.all_to_all(out_part, "tensor", split_axis=2, concat_axis=0, tiled=True),
        lax.all_to_all(in_part, "tensor", split_axis=2, concat_axis=0, tiled=True),
    )
    mixed = jnp.sum(out_pieces.astype(jnp.float32), axis=0).astype(jnp.bfloat16)
    input_grad = jnp.sum(in_pieces.astype(jnp.float32), axis=0).astype(jnp.bfloat16)
    up_sum, down_sum = (
        lax.psum_scatter(
            up_term.astype(jnp.bfloat16), "dp", scatter_dimension=1, tiled=True
        ).astype(jnp.float32),
        lax.psum_scatter(
            down_term.astype(jnp.bfloat16), "dp", scatter_dimension=1, tiled=True
        ).astype(jnp.float32),
    )
    up_grad = up_sum.astype(jnp.bfloat16)
    down_grad = down_sum.astype(jnp.bfloat16)
    return (mixed, input_grad, gate_grad, up_grad, down_grad)


def solution(mesh):
    placed = (
        P("dp", "tensor"),
        P("dp", "tensor"),
        P("tensor", None, None, None),
        P(None, "tensor"),
        P("tensor", None, None, None),
        P(),
        P(),
        P("dp", "tensor"),
    )
    return jax.shard_map(
        shards,
        mesh=mesh,
        in_specs=placed,
        out_specs=(
            P("dp", "tensor"),
            P("dp", "tensor"),
            P("dp", "tensor"),
            P("tensor", "dp", None, None),
            P("tensor", "dp", None, None),
        ),
        check_vma=False,
    )
```

profile of v0, /device:TPU:2, one launch (start us, length us, event | category | flops | bytes accessed | tf_op | source)
XLA Modules:
  0.0 517.0 jit_solution(11576796951660111175)
XLA Ops:
  7.2 1.6 copy.130
  8.9 1.5 copy.121
  10.5 0.7 fusion.58
  12.4 0.8 select_reduce_fusion
  14.0 1.0 scatter_custom_fusion
  14.9 0.8 copy.115
  17.3 1.0 scatter_custom_fusion.1
  18.4 79.6 %all-gather.9.cloned.1.call-done = bf16[128,4096]{0,1:T(8,128)(2,1)} async-done(((bf16[128,128]{0,1:T(8,128)(2,1)}), bf16[128,4096]{0,1:T(8,128)(2,1)}) %all-gather.9.cloned.1.call-update) | async-done | bytes 1048592 | tf_op jit(solution)/shard_map/all_gather | solution.py:46
  98.0 1.6 copy.131
  99.6 2.2 gather_fusion.5
  101.8 3.8 convolution_bitcast_fusion.1
  105.7 3.8 fusion.48
  109.5 0.8 copy.146
  111.6 1.4 scatter_custom_fusion.2
  115.2 66.1 %all-gather.5.cloned.1.call-done = bf16[128,4096]{0,1:T(8,128)(2,1)} async-done(((bf16[128,128]{0,1:T(8,128)(2,1)}), bf16[128,4096]{0,1:T(8,128)(2,1)}) %all-gather.5.cloned.1.call-update) | async-done | bytes 1048592 | tf_op jit(solution)/shard_map/all_gather | solution.py:45
  181.2 1.6 copy.122
  182.9 2.2 gather_fusion.2
  185.0 4.3 convolution_bitcast_fusion.3
  189.4 80.9 %all-gather.11.cloned.1.call-done = bf16[128,16384]{0,1:T(8,128)(2,1)} async-done(((bf16[128,512]{0,1:T(8,128)(2,1)}), bf16[128,16384]{0,1:T(8,128)(2,1)}) %all-gather.11.cloned.1.call-update) | async-done | bytes 4194320 | tf_op jit(solution)/shard_map/all_gather | solution.py:88
  270.3 6.4 %copy.134 = bf16[128,128,128]{2,0,1:T(8,128)(2,1)} copy(bf16[128,128,128]{0,2,1:T(8,128)(2,1)} %bitcast.106) | data formatting | bytes 8388608 | tf_op jit(solution)/shard_map/reshape | solution.py:28
  276.7 2.8 gather_fusion.6
  279.4 6.0 %fusion.54 = (bf16[128,4,128]{2,1,0:T(4,128)(2,1)S(1)}, bf16[128,4,128]{2,1,0:T(4,128)(2,1)S(1)}, bf16[128,4,128]{2,1,0:T(4,128)(2,1)S(1)}) fusion(f32[128,4,128]{2,1,0:T(4,128)S(1)} %reshape.234, bf16[4,128,128]{2,1,0:T(8,128)(2,1)S(1)} %gather_fusion.6, pred[4]{0:T(512)(128)(4,1)S(1)} %copy-done.17, pred[4]{0:T(512)(128)(4,1)S(1)} %copy-done.16, ...), kind=kOutput, calls=%fused_computation.55 | convolution fusion | flops 51511552 | bytes 4981000 | tf_op jit(solution)/shard_map/nkc,ks->nsc/dot_general | solution.py:57
  285.5 0.8 copy.145
  286.4 2.2 gather_fusion.7
  288.6 4.6 convert_bitcast_fusion.1
  293.9 5.2 %convolution_bitcast_fusion = f32[128,64,128]{2,0,1:T(8,128)} fusion(bf16[1,64,128,128]{3,2,1,0:T(8,128)(2,1)S(1)} %copy-done, bf16[64,128,128]{2,1,0:T(8,128)(2,1)} %gather_fusion.7, pred[64]{0:T(512)(128)(4,1)S(1)} %copy-done.6), kind=kOutput, calls=%fused_computation.19 | convolution fusion | flops 269484032 | bytes 8388672 | tf_op jit(solution)/shard_map/nkc,kbc->nkb/dot_general | solution.py:97
  299.1 72.1 %all-gather.7.cloned.1.call-done = bf16[128,16384]{0,1:T(8,128)(2,1)} async-done(((bf16[128,512]{0,1:T(8,128)(2,1)}), bf16[128,16384]{0,1:T(8,128)(2,1)}) %all-gather.7.cloned.1.call-update) | async-done | bytes 4194320 | tf_op jit(solution)/shard_map/all_gather | solution.py:69
  371.2 6.5 %copy.125 = bf16[128,128,128]{2,0,1:T(8,128)(2,1)} copy(bf16[128,128,128]{0,2,1:T(8,128)(2,1)} %bitcast.107) | data formatting | bytes 8388608 | tf_op jit(solution)/shard_map/reshape | solution.py:28
  377.7 2.8 gather_fusion.3
  380.6 2.1 gather_fusion.4
  382.8 4.6 convert_bitcast_fusion
  387.9 6.1 %fusion.36 = bf16[128,32,128]{2,1,0:T(8,128)(2,1)S(1)} fusion(f32[128,64,128]{2,0,1:T(8,128)} %convolution_bitcast_fusion, s32[64]{0:T(128)S(1)} %copy-done.14), kind=kOutput, calls=%fused_computation.45 | convolution fusion | flops 403179520 | bytes 5243136 | tf_op jit(solution)/shard_map/nkb,kr->nrb/dot_general | solution.py:98
  394.5 2.8 copy.138
  397.9 22.4 %reduce.15 = bf16[4096,128]{1,0:T(8,128)(2,1)S(1)} reduce(bf16[4096,1,128]{2,1,0:T(2,128)(2,1)S(1)} %bitcast.102, bf16[]{:T(256)} %broadcast.484), dimensions={1}, to_apply=%bitcast.95.reduce_sub_computation | reduce | bytes 2097154
  420.3 1.1 reshape.359
  421.4 7.0 %all-to-all-start.1 = ((bf16[32,2,8192]{2,1,0:T(2,128)(2,1)}), bf16[32,2,8192]{2,1,0:T(2,128)(2,1)S(1)}, u32[]{:S(2)}, u32[]{:S(2)}) async-start(bf16[32,2,8192]{2,1,0:T(2,128)(2,1)} %reshape.359), calls=%async_computation.1 | async-start | bytes 2097152 | tf_op jit(solution)/shard_map/all_to_all | solution.py:105
  428.4 2.4 convolution_bitcast_fusion.2
  430.8 4.1 fusion.39
  434.9 1.3 reshape.228
  436.2 5.0 copy.129
  441.2 23.4 %reduce.14 = bf16[4096,128]{1,0:T(8,128)(2,1)} reduce(bf16[4096,1,128]{2,1,0:T(2,128)(2,1)S(1)} %bitcast.103, bf16[]{:T(256)} %broadcast.484), dimensions={1}, to_apply=%bitcast.93.reduce_sub_computation | reduce | bytes 2097154
  464.6 2.1 reshape.357
  466.7 9.8 %all-to-all-start = ((bf16[32,2,8192]{2,1,0:T(2,128)(2,1)}), bf16[32,2,8192]{2,1,0:T(2,128)(2,1)}, u32[]{:S(2)}, u32[]{:S(2)}) async-start(bf16[32,2,8192]{2,1,0:T(2,128)(2,1)} %reshape.357), calls=%async_computation | async-start | bytes 2097152 | tf_op jit(solution)/shard_map/all_to_all | solution.py:104
  477.3 1.0 reshape.360
  478.6 0.7 copy.142
  479.3 22.0 %all-to-all-done = bf16[32,2,8192]{2,1,0:T(2,128)(2,1)} async-done(((bf16[32,2,8192]{2,1,0:T(2,128)(2,1)}), bf16[32,2,8192]{2,1,0:T(2,128)(2,1)}, u32[]{:S(2)}, u32[]{:S(2)}) %all-to-all-start) | async-done | bytes 1048608 | tf_op jit(solution)/shard_map/all_to_all | solution.py:104
  501.3 5.8 %reshape.358 = bf16[4096,1,128]{2,1,0:T(2,128)(2,1)} reshape(bf16[32,2,8192]{2,1,0:T(2,128)(2,1)} %all-to-all-done) | data formatting | bytes 2097152
  507.1 1.9 copy.147
  (100 shorter events, 11.4 us)
Async XLA Ops:
  7.2 177.9 %copy-start = (bf16[1,64,128,128]{3,2,1,0:T(8,128)(2,1)S(1)}, bf16[1,64,128,128]{3,2,1,0:T(8,128)(2,1)}, u32[]{:S(2)}) copy-start(bf16[1,64,128,128]{3,2,1,0:T(8,128)(2,1)} %param.16) | copy-start | bytes 6291460
  7.2 90.8 %all-gather.9.cloned.1.call-start = ((), (), s32[]{:S(2)}) async-start(), calls=%async_computation.6 | async-start | bytes 1081344 | tf_op jit(solution)/shard_map/all_gather | solution.py:46
  8.9 172.4 %all-gather.5.cloned.1.call-start = ((), (), s32[]{:S(2)}) async-start(), calls=%async_computation.4 | async-start | bytes 1081344 | tf_op jit(solution)/shard_map/all_gather | solution.py:45
  10.4 259.9 %all-gather.11.cloned.1.call-start = ((), (), s32[]{:S(2)}) async-start(), calls=%async_computation.7 | async-start | bytes 4325376 | tf_op jit(solution)/shard_map/all_gather | solution.py:88
  18.3 83.5 %copy-start.11 = (s32[64]{0:T(128)}, s32[64]{0:T(128)S(1)}, u32[]{:S(2)}) copy-start(s32[64]{0:T(128)S(1)} %get-tuple-element.20) | copy-start | bytes 772
  18.3 87.3 %copy-start.4 = (s32[64]{0:T(128)}, s32[64]{0:T(128)S(1)}, u32[]{:S(2)}) copy-start(s32[64]{0:T(128)S(1)} %get-tuple-element.33) | copy-start | bytes 772
  105.6 4.7 copy-start.9
  105.7 5.0 copy-start.3
  110.3 260.9 %all-gather.7.cloned.1.call-start = ((), (), s32[]{:S(2)}) async-start(), calls=%async_computation.5 | async-start | bytes 4325376 | tf_op jit(solution)/shard_map/all_gather | solution.py:69
  114.6 0.5 copy-start.13
  114.6 70.4 %copy-start.7 = (pred[64]{0:T(512)(128)(4,1)}, pred[64]{0:T(512)(128)(4,1)S(1)}, u32[]{:S(2)}) copy-start(pred[64]{0:T(512)(128)(4,1)S(1)} %get-tuple-element.38) | copy-start | bytes 196
  270.3 9.2 %copy-start.15 = (s32[64]{0:T(128)S(1)}, s32[64]{0:T(128)}, u32[]{:S(2)}) copy-start(s32[64]{0:T(128)} %get-tuple-element.14) | copy-start | bytes 772
  270.3 9.2 %copy-start.16 = (pred[4]{0:T(512)(128)(4,1)S(1)}, pred[4]{0:T(512)(128)(4,1)}, u32[]{:S(2)}) copy-start(pred[4]{0:T(512)(128)(4,1)} %get-tuple-element.15) | copy-start | bytes 16
  270.3 9.2 %copy-start.17 = (pred[4]{0:T(512)(128)(4,1)S(1)}, pred[4]{0:T(512)(128)(4,1)}, u32[]{:S(2)}) copy-start(pred[4]{0:T(512)(128)(4,1)} %get-tuple-element.17) | copy-start | bytes 16
  286.3 223.6 %reduce-scatter.3.cloned.1.call-start = ((), (), s32[]{:S(2)}) async-start(), calls=%async_computation.8 | async-start | bytes 2228224 | tf_op jit(solution)/shard_map/reduce_scatter | solution.py:110
  286.4 2.2 copy-start.6
  286.4 2.2 copy-start.8
  293.2 0.7 copy-start.10
  293.2 0.7 copy-start.5
  293.2 216.7 %reduce-scatter.5.cloned.1.call-start = ((), (), s32[]{:S(2)}) async-start(), calls=%async_computation.9 | async-start | bytes 2228224 | tf_op jit(solution)/shard_map/reduce_scatter | solution.py:113
  387.3 0.6 copy-start.14
  420.2 8.2 %copy-start.2 = (bf16[64,128,128]{2,1,0:T(8,128)(2,1)S(1)}, bf16[64,128,128]{2,1,0:T(8,128)(2,1)}, u32[]{:S(2)}) copy-start(bf16[64,128,128]{2,1,0:T(8,128)(2,1)} %gather_fusion.4) | copy-start | bytes 6291460
  421.4 45.4 %all-to-all-start.1 = ((bf16[32,2,8192]{2,1,0:T(2,128)(2,1)}), bf16[32,2,8192]{2,1,0:T(2,128)(2,1)S(1)}, u32[]{:S(2)}, u32[]{:S(2)}) async-start(bf16[32,2,8192]{2,1,0:T(2,128)(2,1)} %reshape.359), calls=%async_computation.1 | async-start | bytes 2097152 | tf_op jit(solution)/shard_map/all_to_all | solution.py:105
  428.4 2.4 copy-start.12
  466.7 34.6 %all-to-all-start = ((bf16[32,2,8192]{2,1,0:T(2,128)(2,1)}), bf16[32,2,8192]{2,1,0:T(2,128)(2,1)}, u32[]{:S(2)}, u32[]{:S(2)}) async-start(bf16[32,2,8192]{2,1,0:T(2,128)(2,1)} %reshape.357), calls=%async_computation | async-start | bytes 2097152 | tf_op jit(solution)/shard_map/all_to_all | solution.py:104
  507.1 2.8 copy-start.1
Sparse Core Ops, SparseCore 0:
  11.8 86.1 all-gather.8
  101.7 79.5 all-gather.4
  185.0 85.2 all-gather.10
  286.4 84.7 all-gather.6
  374.4 59.0 reduce-scatter.2
  436.8 61.4 reduce-scatter.4
where the time goes:
time: 525 us; the launch traced here: 517 us
  waiting for transfers between devices  321 us (61%)
  local copies, waits for them, and re-layouts  67 us (13%)
  other arithmetic  52.4 us (10%)
  matrix products  44.8 us (9%)
  starting transfers between devices  17.1 us (3%)
  between operations  14.8 us (3%)
    all_gather x1, waiting for transfers between devices, shards(): lax.all_gather(dh_owned, 'tensor', axis=1, tiled=True)  80.9 us
    all_gather x1, waiting for transfers between devices, shards(): lax.all_gather(cotangent, 'tensor', axis=1, tiled=True)  79.6 us
    all_gather x1, waiting for transfers between devices, shards(): lax.all_gather(hidden, 'tensor', axis=1, tiled=True)  72.1 us
    all_gather x1, waiting for transfers between devices, shards(): lax.all_gather(tokens, 'tensor', axis=1, tiled=True)  66.1 us
    unnamed x2, other arithmetic  45.8 us
    all_to_all x1, waiting for transfers between devices, shards(): lax.all_to_all(out_part, 'tensor', split_axis=2, concat_axis=0, tiled=True)  22 us
    unnamed x50, local copies, waits for them, and re-layouts  20.5 us
    reshape x2, local copies, waits for them, and re-layouts, picker(): shaped = segment.reshape(segment.shape[0], block_count, block)  12.9 us
  transfers between devices with their start and end apart: 8, of which 5 were waited for; matrix products, arithmetic and copies ran while one was open for 28% of the time, Pallas kernels for 0%

commit v1 on v0

--- a/solution.py
+++ b/solution.py
@@ -1,7 +1,18 @@
+import functools
 import jax
 import jax.numpy as jnp
 from jax import lax
 from jax.sharding import PartitionSpec as P
+
+
+def spread_the_panels(in_array, mesh_ax, ndim_at):
+    clean = jnp.stack([in_array for _ in range(jax.lax.axis_size(mesh_ax))])
+    z_new = jax.lax.all_to_all(clean, mesh_ax, 0, 0)
+    formed = jnp.concatenate(z_new, axis=ndim_at)
+    return formed
+
+
+settle_the_lots_all = functools.partial(spread_the_panels, mesh_ax="tensor", ndim_at=1)
 
 
 def kept_positions(marked, total):
@@ -43,7 +54,7 @@
     highest = lax.Precision.HIGHEST
     x_full, dy_full = (
         lax.all_gather(tokens, "tensor", axis=1, tiled=True),
-        lax.all_gather(cotangent, "tensor", axis=1, tiled=True),
+        settle_the_lots_all(cotangent),
     )
     token_blocks = x_full.reshape(token_count, blocks_wide, block)
     cot_blocks = dy_full.reshape(token_count, blocks_wide, block)

time: 525 us -> 442 us (0.84)
  waiting for transfers between devices: 321 us -> 229 us
  starting transfers between devices: 17.1 us -> 30.5 us
    all_gather x1 -> x0, waiting for transfers between devices: 79.6 us -> none  [shards(): lax.all_gather(cotangent, 'tensor', axis=1, tiled=True)]
    all_gather x1, waiting for transfers between devices: 66.1 us -> 30.4 us  [shards(): lax.all_gather(tokens, 'tensor', axis=1, tiled=True)]
    all_to_all x0 -> x1, waiting for transfers between devices: none -> 23.7 us  [spread_the_panels(): z_new = jax.lax.all_to_all(clean, mesh_ax, 0, 0)]
    all_to_all x0 -> x1, starting transfers between devices: none -> 13.5 us  [spread_the_panels(): z_new = jax.lax.all_to_all(clean, mesh_ax, 0, 0)]
    unnamed x50 -> x53, local copies, waits for them, and re-layouts: 20.5 us -> 18.7 us
  transfers between devices with their start and end apart: 8 -> 8, of which waited for: 5 -> 5; matrix products, arithmetic and copies ran while one was open for 28% -> 32% of each run, Pallas kernels for 0% -> 0%
where the time goes in v1:
time: 442 us; the launch traced here: 435 us
  waiting for transfers between devices  229 us (52%)
  local copies, waits for them, and re-layouts  65.6 us (15%)
  other arithmetic  49.8 us (11%)
  matrix products  44.8 us (10%)
  starting transfers between devices  30.5 us (7%)
  between operations  14.5 us (3%)
    all_gather x1, waiting for transfers between devices, shards(): lax.all_gather(dh_owned, 'tensor', axis=1, tiled=True)  80.9 us
    all_gather x1, waiting for transfers between devices, shards(): lax.all_gather(hidden, 'tensor', axis=1, tiled=True)  72.2 us
    unnamed x2, other arithmetic  45.8 us
    all_gather x1, waiting for transfers between devices, shards(): lax.all_gather(tokens, 'tensor', axis=1, tiled=True)  30.4 us
    all_to_all x1, waiting for transfers between devices, spread_the_panels(): z_new = jax.lax.all_to_all(clean, mesh_ax, 0, 0)  23.7 us
    all_to_all x1, waiting for transfers between devices, shards(): lax.all_to_all(out_part, 'tensor', split_axis=2, concat_axis=0, tiled=True)  22 us
    unnamed x53, local copies, waits for them, and re-layouts  18.7 us
    all_to_all x1, starting transfers between devices, spread_the_panels(): z_new = jax.lax.all_to_all(clean, mesh_ax, 0, 0)  13.5 us
  transfers between devices with their start and end apart: 8, of which 5 were waited for; matrix products, arithmetic and copies ran while one was open for 32% of the time, Pallas kernels for 0%

profile of v1, /device:TPU:2, one launch (start us, length us, event | category | flops | bytes accessed | tf_op | source)
XLA Modules:
  0.0 434.5 jit_solution(12245935906272836593)
XLA Ops:
  7.2 1.6 copy.115
  8.9 2.0 stack.2
  10.9 13.5 %all-to-all-start.1 = ((bf16[32,128,128]{2,1,0:T(8,128)(2,1)}), bf16[32,128,128]{2,1,0:T(8,128)(2,1)S(1)}, u32[]{:S(2)}, u32[]{:S(2)}) async-start(bf16[32,128,128]{2,1,0:T(8,128)(2,1)} %stack.2), calls=%async_computation.1 | async-start | bytes 2097152 | tf_op jit(solution)/shard_map/all_to_all | solution.py:10
  25.3 1.0 scatter_custom_fusion
  27.9 1.0 scatter_custom_fusion.1
  29.5 23.7 %all-to-all-done.1 = bf16[32,128,128]{2,1,0:T(8,128)(2,1)S(1)} async-done(((bf16[32,128,128]{2,1,0:T(8,128)(2,1)}), bf16[32,128,128]{2,1,0:T(8,128)(2,1)S(1)}, u32[]{:S(2)}, u32[]{:S(2)}) %all-to-all-start.1) | async-done | bytes 1048608 | tf_op jit(solution)/shard_map/all_to_all | solution.py:10
  53.2 2.2 gather_fusion.5
  55.3 3.8 convolution_bitcast_fusion.1
  59.2 3.8 fusion.48
  63.0 0.8 copy.138
  64.4 1.4 scatter_custom_fusion.2
  65.9 0.6 gather_fusion.1
  68.7 30.4 %all-gather.4.cloned.1.call-done = bf16[128,4096]{0,1:T(8,128)(2,1)} async-done(((bf16[128,128]{0,1:T(8,128)(2,1)}), bf16[128,4096]{0,1:T(8,128)(2,1)}) %all-gather.4.cloned.1.call-update) | async-done | bytes 1048592 | tf_op jit(solution)/shard_map/all_gather | solution.py:56
  99.1 1.6 copy.116
  100.7 2.2 gather_fusion.2
  102.9 4.3 convolution_bitcast_fusion.3
  107.2 80.9 %all-gather.8.cloned.1.call-done = bf16[128,16384]{0,1:T(8,128)(2,1)} async-done(((bf16[128,512]{0,1:T(8,128)(2,1)}), bf16[128,16384]{0,1:T(8,128)(2,1)}) %all-gather.8.cloned.1.call-update) | async-done | bytes 4194320 | tf_op jit(solution)/shard_map/all_gather | solution.py:99
  188.1 6.4 %copy.126 = bf16[128,128,128]{2,0,1:T(8,128)(2,1)} copy(bf16[128,128,128]{0,2,1:T(8,128)(2,1)} %bitcast.110) | data formatting | bytes 8388608 | tf_op jit(solution)/shard_map/reshape | solution.py:39
  194.5 2.8 gather_fusion.6
  197.3 6.0 %fusion.54 = (bf16[128,4,128]{2,1,0:T(4,128)(2,1)S(1)}, bf16[128,4,128]{2,1,0:T(4,128)(2,1)S(1)}, bf16[128,4,128]{2,1,0:T(4,128)(2,1)S(1)}) fusion(f32[128,4,128]{2,1,0:T(4,128)S(1)} %reshape.236, bf16[4,128,128]{2,1,0:T(8,128)(2,1)S(1)} %gather_fusion.6, pred[4]{0:T(512)(128)(4,1)S(1)} %copy-done.19, pred[4]{0:T(512)(128)(4,1)S(1)} %copy-done.18, ...), kind=kOutput, calls=%fused_computation.55 | convolution fusion | flops 51511552 | bytes 4981000 | tf_op jit(solution)/shard_map/nkc,ks->nsc/dot_general | solution.py:68
  203.4 0.8 copy.137
  204.3 2.2 gather_fusion.7
  206.5 4.6 %convert_bitcast_fusion.1 = bf16[1,64,128,128]{3,2,1,0:T(8,128)(2,1)} fusion(bf16[64,128,128]{2,1,0:T(8,128)(2,1)} %gather_fusion.2, pred[64]{0:T(512)(128)(4,1)S(1)} %copy-done.10, bf16[64,128,128]{2,1,0:T(8,128)(2,1)} %gather_fusion.7, pred[64]{0:T(512)(128)(4,1)S(1)} %copy-done.8), kind=kOutput, calls=%fused_computation.38 | convolution fusion | flops 271581184 | bytes 6291584 | tf_op jit(solution)/shard_map/nkb,nkc->kbc/dot_general | solution.py:111
  211.7 5.2 %convolution_bitcast_fusion = f32[128,64,128]{2,0,1:T(8,128)} fusion(bf16[1,64,128,128]{3,2,1,0:T(8,128)(2,1)S(1)} %copy-done, bf16[64,128,128]{2,1,0:T(8,128)(2,1)} %gather_fusion.7, pred[64]{0:T(512)(128)(4,1)S(1)} %copy-done.8), kind=kOutput, calls=%fused_computation.19 | convolution fusion | flops 269484032 | bytes 8388672 | tf_op jit(solution)/shard_map/nkc,kbc->nkb/dot_general | solution.py:108
  216.9 72.2 %all-gather.6.cloned.1.call-done = bf16[128,16384]{0,1:T(8,128)(2,1)} async-done(((bf16[128,512]{0,1:T(8,128)(2,1)}), bf16[128,16384]{0,1:T(8,128)(2,1)}) %all-gather.6.cloned.1.call-update) | async-done | bytes 4194320 | tf_op jit(solution)/shard_map/all_gather | solution.py:80
  289.1 6.5 %copy.119 = bf16[128,128,128]{2,0,1:T(8,128)(2,1)} copy(bf16[128,128,128]{0,2,1:T(8,128)(2,1)} %bitcast.111) | data formatting | bytes 8388608 | tf_op jit(solution)/shard_map/reshape | solution.py:39
  295.6 2.8 gather_fusion.3
  298.5 2.1 gather_fusion.4
  300.6 4.6 %convert_bitcast_fusion = bf16[1,64,128,128]{3,2,1,0:T(8,128)(2,1)} fusion(bf16[64,128,128]{2,1,0:T(8,128)(2,1)} %gather_fusion.4, pred[64]{0:T(512)(128)(4,1)S(1)} %get-tuple-element.32, bf16[64,128,128]{2,1,0:T(8,128)(2,1)} %gather_fusion.5, pred[64]{0:T(512)(128)(4,1)S(1)} %get-tuple-element.19), kind=kOutput, calls=%fused_computation.37 | convolution fusion | flops 271581184 | bytes 6291584 | tf_op jit(solution)/shard_map/nkb,nkc->kbc/dot_general | solution.py:89
  305.8 6.1 %fusion.36 = bf16[128,32,128]{2,1,0:T(8,128)(2,1)S(1)} fusion(f32[128,64,128]{2,0,1:T(8,128)} %convolution_bitcast_fusion, s32[64]{0:T(128)S(1)} %copy-done.16), kind=kOutput, calls=%fused_computation.45 | convolution fusion | flops 403179520 | bytes 5243136 | tf_op jit(solution)/shard_map/nkb,kr->nrb/dot_general | solution.py:109
  312.4 2.8 copy.130
  315.7 22.4 %reduce.15 = bf16[4096,128]{1,0:T(8,128)(2,1)S(1)} reduce(bf16[4096,1,128]{2,1,0:T(2,128)(2,1)S(1)} %bitcast.106, bf16[]{:T(256)} %broadcast.486), dimensions={1}, to_apply=%bitcast.95.reduce_sub_computation | reduce | bytes 2097154
  338.1 1.1 reshape.361
  339.2 7.0 %all-to-all-start.2 = ((bf16[32,2,8192]{2,1,0:T(2,128)(2,1)}), bf16[32,2,8192]{2,1,0:T(2,128)(2,1)S(1)}, u32[]{:S(2)}, u32[]{:S(2)}) async-start(bf16[32,2,8192]{2,1,0:T(2,128)(2,1)} %reshape.361), calls=%async_computation.2 | async-start | bytes 2097152 | tf_op jit(solution)/shard_map/all_to_all | solution.py:116
  346.3 2.4 convolution_bitcast_fusion.2
  348.7 4.1 fusion.39
  352.7 1.3 reshape.230
  354.0 5.0 %copy.123 = bf16[1,128,4096]{1,0,2:T(2,128)(2,1)S(1)} copy(bf16[1,128,4096]{2,1,0:T(8,128)(2,1)} %reshape.230) | data formatting | bytes 2097152 | tf_op jit(solution)/shard_map/reshape | solution.py:87
  359.1 23.4 %reduce.14 = bf16[4096,128]{1,0:T(8,128)(2,1)} reduce(bf16[4096,1,128]{2,1,0:T(2,128)(2,1)S(1)} %bitcast.107, bf16[]{:T(256)} %broadcast.486), dimensions={1}, to_apply=%bitcast.93.reduce_sub_computation | reduce | bytes 2097154
  382.4 2.2 reshape.359
  384.6 9.8 %all-to-all-start = ((bf16[32,2,8192]{2,1,0:T(2,128)(2,1)}), bf16[32,2,8192]{2,1,0:T(2,128)(2,1)}, u32[]{:S(2)}, u32[]{:S(2)}) async-start(bf16[32,2,8192]{2,1,0:T(2,128)(2,1)} %reshape.359), calls=%async_computation | async-start | bytes 2097152 | tf_op jit(solution)/shard_map/all_to_all | solution.py:115
  394.4 0.7 copy.177
  395.1 1.0 reshape.362
  396.5 0.7 copy.134
  397.2 22.0 %all-to-all-done = bf16[32,2,8192]{2,1,0:T(2,128)(2,1)} async-done(((bf16[32,2,8192]{2,1,0:T(2,128)(2,1)}), bf16[32,2,8192]{2,1,0:T(2,128)(2,1)}, u32[]{:S(2)}, u32[]{:S(2)}) %all-to-all-start) | async-done | bytes 1048608 | tf_op jit(solution)/shard_map/all_to_all | solution.py:115
  419.2 5.8 %reshape.360 = bf16[4096,1,128]{2,1,0:T(2,128)(2,1)} reshape(bf16[32,2,8192]{2,1,0:T(2,128)(2,1)} %all-to-all-done) | data formatting | bytes 2097152
  425.0 1.9 copy.139
  427.1 0.7 copy.133
  (102 shorter events, 8.8 us)
Async XLA Ops:
  7.2 95.7 %copy-start = (bf16[1,64,128,128]{3,2,1,0:T(8,128)(2,1)S(1)}, bf16[1,64,128,128]{3,2,1,0:T(8,128)(2,1)}, u32[]{:S(2)}) copy-start(bf16[1,64,128,128]{3,2,1,0:T(8,128)(2,1)} %param.16) | copy-start | bytes 6291460
  7.2 17.2 %copy-start.5 = (s32[128]{0:T(128)S(1)}, s32[128]{0:T(128)}, u32[]{:S(2)}) copy-start(s32[128]{0:T(128)} %param.20) | copy-start | bytes 1540
  7.2 19.1 %copy-start.4 = (s32[128,32]{0,1:T(8,128)S(1)}, s32[128,32]{0,1:T(8,128)}, u32[]{:S(2)}) copy-start(s32[128,32]{0,1:T(8,128)} %param.19) | copy-start | bytes 49156
  7.2 91.9 %all-gather.4.cloned.1.call-start = ((), (), s32[]{:S(2)}) async-start(), calls=%async_computation.5 | async-start | bytes 1081344 | tf_op jit(solution)/shard_map/all_gather | solution.py:56
  10.9 42.3 %all-to-all-start.1 = ((bf16[32,128,128]{2,1,0:T(8,128)(2,1)}), bf16[32,128,128]{2,1,0:T(8,128)(2,1)S(1)}, u32[]{:S(2)}, u32[]{:S(2)}) async-start(bf16[32,128,128]{2,1,0:T(8,128)(2,1)} %stack.2), calls=%async_computation.1 | async-start | bytes 2097152 | tf_op jit(solution)/shard_map/all_to_all | solution.py:10
  24.3 163.8 %all-gather.8.cloned.1.call-start = ((), (), s32[]{:S(2)}) async-start(), calls=%async_computation.7 | async-start | bytes 4325376 | tf_op jit(solution)/shard_map/all_gather | solution.py:99
  29.0 0.5 copy-start.13
  29.0 30.2 %copy-start.6 = (s32[64]{0:T(128)}, s32[64]{0:T(128)S(1)}, u32[]{:S(2)}) copy-start(s32[64]{0:T(128)S(1)} %get-tuple-element.33) | copy-start | bytes 772
  59.2 4.7 %copy-start.11 = (s32[32,4]{0,1:T(4,128)S(1)}, s32[32,4]{0,1:T(4,128)}, u32[]{:S(2)}) copy-start(s32[32,4]{0,1:T(4,128)} %param.17) | copy-start | bytes 1540
  59.2 5.0 %copy-start.3 = (bf16[128,512]{1,0:T(8,128)(2,1)S(1)}, bf16[128,512]{1,0:T(8,128)(2,1)}, u32[]{:S(2)}) copy-start(bf16[128,512]{1,0:T(8,128)(2,1)} %param.15) | copy-start | bytes 393220
  63.8 225.3 %all-gather.6.cloned.1.call-start = ((), (), s32[]{:S(2)}) async-start(), calls=%async_computation.6 | async-start | bytes 4325376 | tf_op jit(solution)/shard_map/all_gather | solution.py:80
  67.2 0.5 copy-start.15
  67.2 35.7 %copy-start.9 = (pred[64]{0:T(512)(128)(4,1)}, pred[64]{0:T(512)(128)(4,1)S(1)}, u32[]{:S(2)}) copy-start(pred[64]{0:T(512)(128)(4,1)S(1)} %get-tuple-element.38) | copy-start | bytes 196
  188.1 9.2 %copy-start.17 = (s32[64]{0:T(128)S(1)}, s32[64]{0:T(128)}, u32[]{:S(2)}) copy-start(s32[64]{0:T(128)} %get-tuple-element.14) | copy-start | bytes 772
  188.1 9.2 %copy-start.18 = (pred[4]{0:T(512)(128)(4,1)S(1)}, pred[4]{0:T(512)(128)(4,1)}, u32[]{:S(2)}) copy-start(pred[4]{0:T(512)(128)(4,1)} %get-tuple-element.15) | copy-start | bytes 16
  188.1 9.2 %copy-start.19 = (pred[4]{0:T(512)(128)(4,1)S(1)}, pred[4]{0:T(512)(128)(4,1)}, u32[]{:S(2)}) copy-start(pred[4]{0:T(512)(128)(4,1)} %get-tuple-element.17) | copy-start | bytes 16
  204.2 223.6 %reduce-scatter.3.cloned.1.call-start = ((), (), s32[]{:S(2)}) async-start(), calls=%async_computation.8 | async-start | bytes 2228224 | tf_op jit(solution)/shard_map/reduce_scatter | solution.py:121
  204.3 2.2 copy-start.8
  204.3 2.2 copy-start.10
  211.0 0.7 copy-start.12
  211.0 0.7 copy-start.7
  211.1 216.7 %reduce-scatter.5.cloned.1.call-start = ((), (), s32[]{:S(2)}) async-start(), calls=%async_computation.9 | async-start | bytes 2228224 | tf_op jit(solution)/shard_map/reduce_scatter | solution.py:124
  305.2 0.6 copy-start.16
  338.1 8.2 %copy-start.2 = (bf16[64,128,128]{2,1,0:T(8,128)(2,1)S(1)}, bf16[64,128,128]{2,1,0:T(8,128)(2,1)}, u32[]{:S(2)}) copy-start(bf16[64,128,128]{2,1,0:T(8,128)(2,1)} %gather_fusion.4) | copy-start | bytes 6291460
  339.2 45.4 %all-to-all-start.2 = ((bf16[32,2,8192]{2,1,0:T(2,128)(2,1)}), bf16[32,2,8192]{2,1,0:T(2,128)(2,1)S(1)}, u32[]{:S(2)}, u32[]{:S(2)}) async-start(bf16[32,2,8192]{2,1,0:T(2,128)(2,1)} %reshape.361), calls=%async_computation.2 | async-start | bytes 2097152 | tf_op jit(solution)/shard_map/all_to_all | solution.py:116
  346.3 2.4 copy-start.14
  384.6 34.6 %all-to-all-start = ((bf16[32,2,8192]{2,1,0:T(2,128)(2,1)}), bf16[32,2,8192]{2,1,0:T(2,128)(2,1)}, u32[]{:S(2)}, u32[]{:S(2)}) async-start(bf16[32,2,8192]{2,1,0:T(2,128)(2,1)} %reshape.359), calls=%async_computation | async-start | bytes 2097152 | tf_op jit(solution)/shard_map/all_to_all | solution.py:115
  425.0 2.8 copy-start.1
Sparse Core Ops, SparseCore 0:
  11.8 87.2 all-gather.3
  102.8 85.2 all-gather.7
  204.3 84.7 all-gather.5
  292.3 59.0 reduce-scatter.2
  354.7 61.5 reduce-scatter.4
